TPU v7x, 256 devices: a whole 4x4x8 slice. The times are simulated.
256 devices in a mesh: pix: 64 (over z, y, core), lat: 4 (over x).
Axes of the slice: x: 4, y: 4, z: 8, core: 2. Of those that a mesh axis runs over, the one named last changes fastest.
Arguments:
- latents: float32 [2048, 512], P('lat'), as said below
- pixel_keys: float32 [32768, 512], P('pix'), as said below
- pixel_values: float32 [32768, 512], P('pix'), may hold values from -6 to 6
- norm_gain: float32 [512], replicated, may hold values from 0.1 to 1.9
- w_key: float32 [512, 512], replicated, may hold values from -0.25 to 0.25
- w_value: float32 [512, 512], replicated, may hold values from -0.25 to 0.25
- pixel_queries: float32 [32768, 512], P('pix'), as said below
Outputs:
- latent_state: float32 [2048, 512], P('lat')
- pixel_out: float32 [32768, 512], P('pix')
Inputs may be any that keep to these rules, and one draw needn't show every extreme that they name: Real-valued latents. `pixel_keys`: Real-valued keys. `pixel_queries`: Real-valued queries.
All inputs are finite; a program needn't handle non-finite values.
Results may differ from a plain program's by a relative error of at most 0.0003.
Values sent between devices are 32-bit elements; how exact they have to be, the bound alone decides.
A program may use at most 64 MiB of HBM per device.

v0:
```python
import math

import jax
import jax.numpy as jnp
from jax import lax
from jax.sharding import PartitionSpec as P


def sent_to_all(value, axis):
    size = lax.axis_size(axis)
    return lax.all_to_all(
        jnp.broadcast_to(value[None], (size, *value.shape)), axis, 0, 0, tiled=True
    )


def over_copies(value, axis):
    return sent_to_all(value, axis).max(axis=0)


def cut_along(value, dim, size):
    dims = value.shape
    pieces = value.reshape(*dims[:dim], size, dims[dim] // size, *dims[dim + 1 :])
    return jnp.moveaxis(pieces, dim, 0)


def summed_on_arrival(value, axis, dim):
    size = lax.axis_size(axis)
    pieces = lax.all_to_all(cut_along(value, dim, size), axis, 0, 0, tiled=True)
    return jnp.sum(pieces, axis=0)


def side_by_side(arrays, axis, dim, along):
    widths = [math.prod(a.shape[along:]) for a in arrays]
    both = jnp.concatenate(
        [a.reshape(*a.shape[:along], w) for a, w in zip(arrays, widths)], axis=along
    )
    filled = summed_on_arrival(both, axis, dim)
    pieces = jnp.split(filled, [sum(widths[:k]) for k in range(1, len(widths))], axis=along)
    return tuple(
        (b.reshape(*filled.shape[:along], *a.shape[along:]) for a, b in zip(arrays, pieces))
    )


def in_one_piece(arrays, axis, dim, along):
    widths = [a.shape[along] for a in arrays]
    both = jnp.concatenate(arrays, axis=along)
    filled = lax.all_gather(both, axis, axis=dim, tiled=True)
    return tuple(jnp.split(filled, [sum(widths[:k]) for k in range(1, len(widths))], axis=along))


def partials(queries, keys, values):
    scores = jnp.dot(queries, keys.T, precision=lax.Precision.HIGHEST) / jnp.sqrt(
        jnp.float32(keys.shape[1])
    )
    top = jnp.max(scores, axis=1)
    weights = jnp.exp(scores - top[:, None])
    total = jnp.sum(weights, axis=1)
    weighted = jnp.dot(weights, values, precision=lax.Precision.HIGHEST)
    return (top, total, weighted)


def project(state, norm_gain, w_key, w_value):
    normed = state / jnp.sqrt(jnp.mean(state * state, axis=1, keepdims=True) + 1e-06) * norm_gain
    keys_new = jnp.dot(normed, w_key, precision=lax.Precision.HIGHEST)
    values_new = jnp.dot(normed, w_value, precision=lax.Precision.HIGHEST)
    return (keys_new, values_new)


def shards(latents, pixel_keys, pixel_values, norm_gain, w_key, w_value, pixel_queries):
    top, total, weighted = partials(latents, pixel_keys, pixel_values)
    best = over_copies(top, "pix")
    rescale = jnp.exp(top - best)
    share_total, share_weighted = side_by_side(
        (total * rescale, weighted * rescale[:, None]), "pix", 0, 1
    )
    count = share_total.shape[0]
    own_rows = lax.dynamic_slice_in_dim(latents, lax.axis_index("pix") * count, count, 0)
    share_state = own_rows + share_weighted / share_total[:, None]
    share_keys, share_values = project(share_state, norm_gain, w_key, w_value)
    latent_state, latent_keys, latent_values = in_one_piece(
        (share_state, share_keys, share_values), "pix", 0, 1
    )
    all_keys, all_values = in_one_piece((latent_keys, latent_values), "lat", 0, 1)
    ptop, ptotal, pweighted = partials(pixel_queries, all_keys, all_values)
    pixel_out = pweighted / ptotal[:, None]
    return (latent_state, pixel_out)


def solution(mesh):
    in_specs = (P("lat", None), P("pix", None), P("pix", None), P(), P(), P(), P("pix", None))
    out_specs = (P("lat", None), P("pix", None))
    return jax.shard_map(shards, mesh=mesh, in_specs=in_specs, out_specs=out_specs, check_vma=False)
```

profile of v0, /device:TPU:1, one launch (start us, length us, event | category | flops | bytes accessed | tf_op | source)
XLA Modules:
  0.0 268.6 jit_solution(1387545714941769349)
XLA Ops:
  7.2 3.6 %fusion.19 = (f32[512]{0:T(512)S(1)}, f32[512,512]{0,1:T(8,128)S(1)}) fusion(f32[512,512]{1,0:T(8,128)} %param.7, f32[512,512]{1,0:T(8,128)} %param.8), kind=kOutput, calls=%fused_computation.29 | convolution fusion | flops 1611136512 | bytes 3147776 | tf_op jit(solution)/shard_map/dot_general | solution.py:52
  10.8 0.7 broadcast_in_dim.2
  11.5 13.2 %all-to-all-start = ((f32[64,1,512]{2,1,0:T(1,128)}), f32[64,1,512]{2,1,0:T(1,128)S(1)}, u32[]{:S(2)}, u32[]{:S(2)}) async-start(f32[64,1,512]{2,1,0:T(1,128)} %broadcast_in_dim.2), calls=%async_computation | async-start | bytes 262144 | tf_op jit(solution)/shard_map/all_to_all | solution.py:11
  24.6 0.2 fusion.11
  24.8 10.9 %all-to-all-done = f32[64,1,512]{2,1,0:T(1,128)S(1)} async-done(((f32[64,1,512]{2,1,0:T(1,128)}), f32[64,1,512]{2,1,0:T(1,128)S(1)}, u32[]{:S(2)}, u32[]{:S(2)}) %all-to-all-start) | async-done | bytes 131104 | tf_op jit(solution)/shard_map/all_to_all | solution.py:11
  35.8 0.1 reduce_max.28
  35.9 0.2 mul.44
  36.1 1.9 fusion.7
  38.1 1.5 pad_maximum_fusion
  39.5 4.5 %all-to-all-start.1 = ((f32[64,8,513]{2,1,0:T(8,128)}), f32[64,8,513]{2,1,0:T(8,128)S(1)}, u32[]{:S(2)}, u32[]{:S(2)}) async-start(f32[64,8,513]{2,1,0:T(8,128)} %pad_maximum_fusion), calls=%async_computation.1 | async-start | bytes 2621440 | tf_op jit(solution)/shard_map/all_to_all | solution.py:28
  44.1 33.7 %all-to-all-done.1 = f32[64,8,513]{2,1,0:T(8,128)S(1)} async-done(((f32[64,8,513]{2,1,0:T(8,128)}), f32[64,8,513]{2,1,0:T(8,128)S(1)}, u32[]{:S(2)}, u32[]{:S(2)}) %all-to-all-start.1) | async-done | bytes 1050656 | tf_op jit(solution)/shard_map/all_to_all | solution.py:28
  77.8 0.1 reduce_sum.37
  77.9 0.1 slice_reduce_fusion
  78.0 0.9 multiply_reduce_fusion.1
  79.0 0.6 fusion.14
  79.6 1.8 fusion.15
  81.4 0.6 pad_maximum_fusion.1
  82.1 75.8 %all-gather.3.cloned.1.call-done = f32[512,1536]{1,0:T(8,128)} async-done(((f32[8,1536]{1,0:T(8,128)}), f32[512,1536]{1,0:T(8,128)}) %all-gather.3.cloned.1.call-update) | async-done | bytes 3145744 | tf_op jit(solution)/shard_map/all_gather | solution.py:47
  157.9 3.3 %concatenate.16 = f32[512,1024]{1,0:T(8,128)} slice(f32[512,1536]{1,0:T(8,128)} %all-gather.3.cloned.1.call-done), slice={[0:512], [512:1536]} | slice | bytes 4194304 | tf_op jit(solution)/shard_map/concatenate | solution.py:46
  161.2 2.3 split.24
  163.5 80.6 %all-gather.5.cloned.1.call-done = f32[2048,1024]{1,0:T(8,128)} async-done(((f32[512,1024]{1,0:T(8,128)}), f32[2048,1024]{1,0:T(8,128)}) %all-gather.5.cloned.1.call-update) | async-done | bytes 8388624 | tf_op jit(solution)/shard_map/all_gather | solution.py:47
  244.1 8.7 %multiply_reduce_fusion = (f32[512]{0:T(512)S(1)}, f32[2048,512]{1,0:T(8,128)S(1)}) fusion(f32[512,512]{1,0:T(8,128)S(1)} %copy-done, f32[2048,1024]{1,0:T(8,128)} %all-gather.5.cloned.1.call-done), kind=kOutput, calls=%fused_computation.5 | convolution fusion | flops 6444547584 | bytes 9439232 | tf_op jit(solution)/shard_map/dot_general | solution.py:52
  252.8 0.8 fusion.4
  253.6 8.2 %fusion.8 = f32[512,512]{1,0:T(8,128)} fusion(f32[2048,1024]{1,0:T(8,128)S(1)} %copy-done.1, f32[2048,512]{1,0:T(8,128)S(1)} %get-tuple-element.9, f32[512]{0:T(512)S(1)} %get-tuple-element.8, f32[512]{0:T(512)S(1)} %fusion.4), kind=kOutput, calls=%fused_computation.13 | convolution fusion | flops 6444810240 | bytes 9441280 | tf_op jit(solution)/shard_map/dot_general | solution.py:58
  (16 shorter events, 0.2 us)
Async XLA Ops:
  7.2 236.9 %copy-start = (f32[512,512]{1,0:T(8,128)S(1)}, f32[512,512]{1,0:T(8,128)}, u32[]{:S(2)}) copy-start(f32[512,512]{1,0:T(8,128)} %param.13) | copy-start | bytes 3145732
  7.2 28.9 %copy-start.2 = (f32[512,512]{1,0:T(8,128)S(1)}, f32[512,512]{1,0:T(8,128)}, u32[]{:S(2)}) copy-start(f32[512,512]{1,0:T(8,128)} %param.9) | copy-start | bytes 3145732
  11.5 24.3 %all-to-all-start = ((f32[64,1,512]{2,1,0:T(1,128)}), f32[64,1,512]{2,1,0:T(1,128)S(1)}, u32[]{:S(2)}, u32[]{:S(2)}) async-start(f32[64,1,512]{2,1,0:T(1,128)} %broadcast_in_dim.2), calls=%async_computation | async-start | bytes 262144 | tf_op jit(solution)/shard_map/all_to_all | solution.py:11
  36.1 42.8 %copy-start.4 = (f32[512]{0:T(512)S(1)}, f32[512]{0:T(512)}, u32[]{:S(2)}) copy-start(f32[512]{0:T(512)} %param.10) | copy-start | bytes 6148
  38.1 40.9 %copy-start.3 = (f32[512,512]{1,0:T(8,128)S(1)}, f32[512,512]{1,0:T(8,128)}, u32[]{:S(2)}) copy-start(f32[512,512]{1,0:T(8,128)} %param.12) | copy-start | bytes 3145732
  39.5 38.3 %all-to-all-start.1 = ((f32[64,8,513]{2,1,0:T(8,128)}), f32[64,8,513]{2,1,0:T(8,128)S(1)}, u32[]{:S(2)}, u32[]{:S(2)}) async-start(f32[64,8,513]{2,1,0:T(8,128)} %pad_maximum_fusion), calls=%async_computation.1 | async-start | bytes 2621440 | tf_op jit(solution)/shard_map/all_to_all | solution.py:28
  44.0 113.9 %all-gather.3.cloned.1.call-start = ((), (), s32[]{:S(2)}) async-start(), calls=%async_computation.2 | async-start | bytes 3194880 | tf_op jit(solution)/shard_map/all_gather | solution.py:47
  82.1 162.0 %all-gather.5.cloned.1.call-start = ((), (), s32[]{:S(2)}) async-start(), calls=%async_computation.3 | async-start | bytes 10485760 | tf_op jit(solution)/shard_map/all_gather | solution.py:47
  244.1 9.5 %copy-start.1 = (f32[2048,1024]{1,0:T(8,128)S(1)}, f32[2048,1024]{1,0:T(8,128)}, u32[]{:S(2)}) copy-start(f32[2048,1024]{1,0:T(8,128)} %all-gather.5.cloned.1.call-done) | copy-start | bytes 25165828
Sparse Core Ops, SparseCore 0:
  82.2 75.7 all-gather.2
  161.3 82.6 all-gather.4
where the time goes:
time: 269 us
  waiting for transfers between devices  201 us (75%)
  matrix products  24.8 us (9%)
  starting transfers between devices  17.7 us (7%)
  between operations  14.2 us (5%)
  local copies, waits for them, and re-layouts  6.61 us (2%)
  other arithmetic  4.21 us (2%)
    all_gather x2, waiting for transfers between devices, in_one_piece(): filled = lax.all_gather(both, axis, axis=dim, tiled=True)  156 us
    all_to_all x1, waiting for transfers between devices, summed_on_arrival(): pieces = lax.all_to_all(cut_along(value, dim, size), axis, 0, 0, tiled=True)  33.7 us
    all_to_all x1, starting transfers between devices, sent_to_all(): lax.all_to_all(jnp.broadcast_to(value[None], (size, *value.shape)), axis,...  13.2 us
    dot_general x2, matrix products, partials(): jnp.dot(queries, keys.T, precision=lax.Precision.HIGHEST)  12.3 us
    all_to_all x1, waiting for transfers between devices, sent_to_all(): lax.all_to_all(jnp.broadcast_to(value[None], (size, *value.shape)), axis,...  10.9 us
    dot_general x2, matrix products, partials(): weighted = jnp.dot(weights, values, precision=lax.Precision.HIGHEST)  10.1 us
  transfers between devices with their start and end apart: 4, of which 4 were waited for; matrix products, arithmetic and copies ran while one was open for 1% of the time, Pallas kernels for 0%

commit v1 on v0

v1 whole, which is shorter than its diff:
```python
import functools

import jax
import jax.numpy as jnp
from jax import lax
from jax.experimental import pallas as pl
from jax.experimental.pallas import tpu as pltpu
from jax.sharding import PartitionSpec as P

MESH = pl.DeviceIdType.MESH
F32, BF16 = jnp.float32, jnp.bfloat16
D = 512
NY, NZ, NX = 4, 8, 4
ROWS = 512
HALF = ROWS // 2
GROUP = 8
TILES = D // 128
SLAB = TILES * NZ * GROUP + 16
PIECE = TILES * GROUP + 16
TOP = TILES * NZ * GROUP
NN = (((1,), (0,)), ((), ()))
NT = (((1,), (1,)), ((), ()))
SCALE = 512.0**-0.5


def split(value):
    high = value.astype(BF16)
    return high, (value - high.astype(F32)).astype(BF16)


def dot3(a, b, dims):
    def one(u, v):
        return lax.dot_general(u, v, dims, preferred_element_type=F32)

    return one(a[0], b[0]) + (one(a[0], b[1]) + one(a[1], b[0]))


def kernel(
    lat_in, keys_in, vals_in, gain_in, wk_in, wv_in, q_in, state_out, pix_out,
    lat, keys, vals, gain, wk, wv, q,
    kh, kl, vh, vl, qh, ql, wvh, wvl,
    slab_send, slab_own, slab_sib, slab_c, slab_r, piece, piece_r,
    g, acc, mx, tot, result,
    in_sem, out_sem, a0s, a0r, a1s, a1r, a2s, a2r, g1s, g1r, g2s, g2r, g3s, g3r, cs, cr,
):
    p = lax.axis_index("pix")
    x = lax.axis_index("lat")
    c = lax.rem(p, 2)
    y = lax.rem(p // 2, NY)
    z = p // (2 * NY)

    def at(zz, yy, cc, xx):
        return ((zz * NY + yy) * 2 + cc, xx)

    sib = at(z, y, 1 - c, x)

    def ypeer(d):
        return at(z, lax.rem(y + d + NY, NY), c, x)

    def zpeer(d):
        return at(lax.rem(z + d + NZ, NZ), y, c, x)

    def xpeer(d):
        return at(z, y, c, lax.rem(x + d + NX, NX))

    loads = []
    for k, (src, dst) in enumerate(
        [(lat_in, lat), (keys_in, keys), (vals_in, vals), (q_in, q), (wk_in, wk), (gain_in, gain), (wv_in, wv)]
    ):
        cp = pltpu.make_async_copy(src, dst, in_sem.at[k])
        cp.start()
        loads.append(cp)

    barrier = pltpu.get_barrier_semaphore()
    peers = (
        [sib]
        + [ypeer(d) for d in range(1, NY)]
        + [zpeer(d) for d in range(1, NZ)]
        + [xpeer(d) for d in range(1, NX)]
    )
    for dev in peers:
        pl.semaphore_signal(barrier, inc=1, device_id=dev, device_id_type=MESH)

    def remote(src, dst, ss, rs, dev):
        return pltpu.make_async_remote_copy(
            src_ref=src, dst_ref=dst, send_sem=ss, recv_sem=rs, device_id=dev, device_id_type=MESH
        )

    started = []

    def send(*args):
        cp = remote(*args)
        cp.start()
        started.append(cp)
        return cp

    lanes = lax.broadcasted_iota(jnp.int32, (GROUP, 128), 1)

    loads[0].wait()
    loads[1].wait()
    kh[...], kl[...] = split(keys[...])

    def first(which, slab):
        lh = split(lat[pl.ds(pl.multiple_of(which * HALF, HALF), HALF), :])
        s = dot3(lh, (kh[...], kl[...]), NT) * SCALE
        top = jnp.max(s, axis=1, keepdims=True)
        w = jnp.exp(s - top)
        total = jnp.sum(w, axis=1, keepdims=True)
        o = dot3(split(w), (vh[...], vl[...]), NN)
        for yy in range(NY):
            tops = jnp.zeros((GROUP, 128), F32)
            totals = jnp.zeros((GROUP, 128), F32)
            for zz in range(NZ):
                r = (zz // 4) * 128 + yy * 32 + (zz % 4) * GROUP
                tops = jnp.where(lanes == zz, top[r : r + GROUP], tops)
                totals = jnp.where(lanes == zz, total[r : r + GROUP], totals)
                for t in range(TILES):
                    slab[yy, (t * NZ + zz) * GROUP : (t * NZ + zz + 1) * GROUP, :] = o[
                        r : r + GROUP, t * 128 : (t + 1) * 128
                    ]
            slab[yy, TOP : TOP + 8, :] = tops
            slab[yy, TOP + 8 : TOP + 16, :] = totals

    loads[2].wait()
    vh[...], vl[...] = split(vals[...])
    first(1 - c, slab_send)
    pl.semaphore_wait(barrier, len(peers))
    order = (1, 3, 2, 0)
    siblings = {}
    for d in order:
        yy = lax.rem(y + d, NY)
        siblings[d] = send(slab_send.at[yy], slab_sib.at[yy], a0s.at[d], a0r.at[d], sib)
    first(c, slab_own)

    to_y = {}
    for d in order:
        yy = lax.rem(y + d, NY)
        siblings[d].wait_recv()
        mo, ms = slab_own[yy, TOP : TOP + 8, :], slab_sib[yy, TOP : TOP + 8, :]
        m = jnp.maximum(mo, ms)
        a, b = jnp.exp(mo - m), jnp.exp(ms - m)
        slab_c[d, TOP : TOP + 8, :] = m
        slab_c[d, TOP + 8 : TOP + 16, :] = (
            a * slab_own[yy, TOP + 8 : TOP + 16, :] + b * slab_sib[yy, TOP + 8 : TOP + 16, :]
        )
        for zz in range(NZ):
            az, bz = a[:, zz : zz + 1], b[:, zz : zz + 1]
            for t in range(TILES):
                r = (t * NZ + zz) * GROUP
                slab_c[d, r : r + GROUP, :] = (
                    az * slab_own[yy, r : r + GROUP, :] + bz * slab_sib[yy, r : r + GROUP, :]
                )
        if d:
            to_y[d] = send(slab_c.at[d], slab_r.at[d], a1s.at[d], a1r.at[d], ypeer(d))

    for k in (3, 4, 5):
        loads[k].wait()
    scaled = dot3(split(q[...]), split(wk[...]), NT) * (gain[...] * SCALE)
    qh[...], ql[...] = split(scaled)

    for d in (1, 3, 2):
        to_y[d].wait_recv()
    parts = [slab_c.at[0]] + [slab_r.at[d] for d in range(1, NY)]
    tops = [s[TOP : TOP + 8, :] for s in parts]
    m = functools.reduce(jnp.maximum, tops)
    scales = [jnp.exp(v - m) for v in tops]
    total = functools.reduce(jnp.add, [s * v[TOP + 8 : TOP + 16, :] for s, v in zip(scales, parts)])
    for zz in range(NZ):
        cols = [s[:, zz : zz + 1] for s in scales]
        for t in range(TILES):
            r = (t * NZ + zz) * GROUP
            piece[zz, t * GROUP : (t + 1) * GROUP, :] = functools.reduce(
                jnp.add, [u * v[r : r + GROUP, :] for u, v in zip(cols, parts)]
            )
        piece[zz, TILES * GROUP : TILES * GROUP + 8, :] = jnp.broadcast_to(m[:, zz : zz + 1], (8, 128))
        piece[zz, TILES * GROUP + 8 : PIECE, :] = jnp.broadcast_to(total[:, zz : zz + 1], (8, 128))

    z_order = (4, 3, 5, 2, 6, 1, 7)
    to_z = {}
    for d in z_order:
        zz = lax.rem(z + d, NZ)
        to_z[d] = send(piece.at[zz], piece_r.at[d], a2s.at[d], a2r.at[d], zpeer(d))
    loads[6].wait()
    wvh[...], wvl[...] = split(wv[...])
    for d in z_order:
        to_z[d].wait_recv()
    parts = [piece.at[z]] + [piece_r.at[d] for d in range(1, NZ)]
    tops = [v[TILES * GROUP : TILES * GROUP + 8, :] for v in parts]
    m = functools.reduce(jnp.maximum, tops)
    scales = [jnp.exp(v - m) for v in tops]
    total = functools.reduce(jnp.add, [s * v[TILES * GROUP + 8 : PIECE, :] for s, v in zip(scales, parts)])
    row = pl.multiple_of(c * HALF + (z // 4) * 128 + y * 32 + lax.rem(z, 4) * GROUP, GROUP)
    for t in range(TILES):
        o = functools.reduce(
            jnp.add, [s * v[t * GROUP : (t + 1) * GROUP, :] for s, v in zip(scales, parts)]
        )
        cols = slice(t * 128, (t + 1) * 128)
        g[x, pl.ds(row, GROUP), cols] = lat[pl.ds(row, GROUP), cols] + o / total

    mine = g.at[x, pl.ds(row, GROUP)]
    gather_z = {d: send(mine, mine, g1s.at[d], g1r.at[d], zpeer(d)) for d in z_order}
    for d in z_order:
        gather_z[d].wait_recv()
    low = g.at[x, pl.ds(pl.multiple_of(c * HALF + y * 32, 32), 32)]
    high = g.at[x, pl.ds(pl.multiple_of(c * HALF + 128 + y * 32, 32), 32)]
    near = (1, 3, 2)
    second = {}
    for d in near:
        second["y", d] = send(low, low, g2s.at[0, d], g2r.at[0, d], ypeer(d))
        second["x", d] = send(high, high, g2s.at[1, d], g2r.at[1, d], xpeer(d))
    for d in near:
        second["y", d].wait_recv()
        second["x", d].wait_recv()

    def low_of(xx, cc):
        return g.at[xx, pl.ds(pl.multiple_of(cc * HALF, HALF), 128)]

    def high_of(yy, cc):
        return g.at[:, pl.ds(pl.multiple_of(cc * HALF + 128 + yy * 32, 32), 32)]

    third = {}
    for d in near:
        third["x", d] = send(low_of(x, c), low_of(x, c), g3s.at[0, d], g3r.at[0, d], xpeer(d))
        third["y", d] = send(high_of(y, c), high_of(y, c), g3s.at[1, d], g3r.at[1, d], ypeer(d))

    acc[...] = jnp.zeros_like(acc)
    tot[...] = jnp.zeros_like(tot)

    def attend(blocks, start):
        n = jnp.concatenate([b.reshape(-1, D) for b in blocks], axis=0)
        n = n * (1.0 / jnp.sqrt(jnp.mean(n * n, axis=1, keepdims=True) + 1e-6))
        nh = split(n)
        s = dot3((qh[...], ql[...]), nh, NT)
        top = jnp.max(s, axis=1, keepdims=True)
        if start:
            m = top
            w = jnp.exp(s - m)
            tot[...] = jnp.broadcast_to(jnp.sum(w, axis=1, keepdims=True), tot.shape)
            acc[...] = dot3(split(w), nh, NN)
        else:
            old = mx[:, 0:1]
            m = jnp.maximum(old, top)
            w = jnp.exp(s - m)
            fade = jnp.exp(old - m)
            tot[...] = tot[...] * fade + jnp.sum(w, axis=1, keepdims=True)
            acc[...] = acc[...] * fade + dot3(split(w), nh, NN)
        mx[...] = jnp.broadcast_to(m, mx.shape)

    def source(kind, d, cc):
        if kind == "x":
            return low_of(lax.rem(x - d + NX, NX), cc)
        return high_of(lax.rem(y - d + NY, NY), cc)

    steps = [("x", 0), ("y", 0), ("x", 1), ("y", 1), ("x", 3), ("y", 3), ("x", 2), ("y", 2)]

    def forward(k):
        kind, d = steps[k]
        if d:
            third[kind, d].wait_recv()
        ref = source(kind, d, c)
        return send(ref, ref, cs.at[k], cr.at[k], sib)

    forwards = {0: forward(0), 1: forward(1)}
    for k, (kind, d) in enumerate(steps):
        if k >= 1 and k + 1 < len(steps):
            forwards[k + 1] = forward(k + 1)
        forwards[k].wait_recv()
        if k == len(steps) - 1:
            save = pltpu.make_async_copy(g.at[x], state_out, out_sem.at[0])
            save.start()
        attend([source(kind, d, 0)[...], source(kind, d, 1)[...]], k == 0)

    o = acc[...] / tot[:, 0:1] * gain[...]
    result[...] = dot3(split(o), (wvh[...], wvl[...]), NN)
    write = pltpu.make_async_copy(result, pix_out, out_sem.at[1])
    write.start()
    for cp in started:
        cp.wait_send()
    save.wait()
    write.wait()


def shards(latents, pixel_keys, pixel_values, norm_gain, w_key, w_value, pixel_queries):
    in_hbm = pl.BlockSpec(memory_space=pltpu.HBM)
    big = pltpu.VMEM((ROWS, D), F32)
    half = pltpu.VMEM((ROWS, D), BF16)
    dma = pltpu.SemaphoreType.DMA
    return pl.pallas_call(
        kernel,
        out_shape=(jax.ShapeDtypeStruct((ROWS, D), F32), jax.ShapeDtypeStruct((ROWS, D), F32)),
        in_specs=[in_hbm] * 7,
        out_specs=(in_hbm, in_hbm),
        scratch_shapes=[
            big, big, big, pltpu.VMEM((1, D), F32), big, big, big,
            half, half, half, half, half, half, half, half,
            pltpu.VMEM((NY, SLAB, 128), F32),
            pltpu.VMEM((NY, SLAB, 128), F32),
            pltpu.VMEM((NY, SLAB, 128), F32),
            pltpu.VMEM((NY, SLAB, 128), F32),
            pltpu.VMEM((NY, SLAB, 128), F32),
            pltpu.VMEM((NZ, PIECE, 128), F32),
            pltpu.VMEM((NZ, PIECE, 128), F32),
            pltpu.VMEM((NX, ROWS, D), F32),
            big,
            pltpu.VMEM((ROWS, 128), F32),
            pltpu.VMEM((ROWS, 128), F32),
            big,
            dma((7,)), dma((2,)),
            dma((NY,)), dma((NY,)), dma((NY,)), dma((NY,)),
            dma((NZ,)), dma((NZ,)), dma((NZ,)), dma((NZ,)),
            dma((2, NY)), dma((2, NY)), dma((2, NY)), dma((2, NY)),
            dma((8,)), dma((8,)),
        ],
        compiler_params=pltpu.CompilerParams(
            collective_id=0, has_side_effects=True, vmem_limit_bytes=48 << 20
        ),
        name="perceiver",
    )(latents, pixel_keys, pixel_values, norm_gain.reshape(1, D), w_key, w_value, pixel_queries)


def solution(mesh):
    in_specs = (P("lat", None), P("pix", None), P("pix", None), P(), P(), P(), P("pix", None))
    out_specs = (P("lat", None), P("pix", None))
    return jax.shard_map(shards, mesh=mesh, in_specs=in_specs, out_specs=out_specs, check_vma=False)
```

time: 269 us -> 70.8 us (0.26)
  waiting for transfers between devices: 201 us -> 0 us
  Pallas kernels: 0 us -> 63.6 us
  matrix products: 24.8 us -> 0 us
  starting transfers between devices: 17.7 us -> 0 us
  between operations: 14.2 us -> 0.65 us
  other arithmetic: 4.21 us -> 0 us
    all_gather x2 -> x0, waiting for transfers between devices: 156 us -> none  [in_one_piece(): filled = lax.all_gather(both, axis, axis=dim, tiled=True)]
    pallas_call x0 -> x1, Pallas kernels: none -> 63.6 us  [shards(): pl.pallas_call(kernel, out_shape=(jax.ShapeDtypeStruct((ROWS, D), F32), j...]
    all_to_all x2 -> x0, waiting for transfers between devices: 44.6 us -> none  [the longest x1 33.7 us: summed_on_arrival(): pieces = lax.all_to_all(cut_along(value, dim, size), axis, 0, 0, tiled=True)]
    dot_general x6 -> x0, matrix products: 24.8 us -> none  [the longest x2 12.3 us: partials(): jnp.dot(queries, keys.T, precision=lax.Precision.HIGHEST)]
    all_to_all x2 -> x0, starting transfers between devices: 17.6 us -> none  [the longest x1 13.2 us: sent_to_all(): lax.all_to_all(jnp.broadcast_to(value[None], (size, *value.shape)), axis,...]
    unnamed x10, local copies, waits for them, and re-layouts: 0.03 us -> 6.29 us
    concatenate x1 -> x0, local copies, waits for them, and re-layouts: 3.26 us -> none  [in_one_piece(): both = jnp.concatenate(arrays, axis=along)]
  transfers between devices with their start and end apart: 4 -> 0, of which waited for: 4 -> 0; matrix products, arithmetic and copies ran while one was open for 1% -> 0% of each run, Pallas kernels for 0% -> 0%
where the time goes in v1:
time: 70.8 us; the launch traced here: 70.5 us
  Pallas kernels  63.6 us (90%)
  local copies, waits for them, and re-layouts  6.29 us (9%)
    pallas_call x1, Pallas kernels, shards(): pl.pallas_call(kernel, out_shape=(jax.ShapeDtypeStruct((ROWS, D), F32), j...  63.6 us
    unnamed x10, local copies, waits for them, and re-layouts  6.29 us

profile of v1, /device:TPU:1, one launch (start us, length us, event | category | flops | bytes accessed | tf_op | source)
XLA Modules:
  0.0 70.5 jit_solution(2501588336291872060)
XLA Ops:
  0.6 0.0 copy-start
  0.6 1.2 %copy-done = f32[512,512]{1,0:T(8,128)S(1)} copy-done((f32[512,512]{1,0:T(8,128)S(1)}, f32[512,512]{1,0:T(8,128)}, u32[]{:S(2)}) %copy-start) | copy-done | bytes 1048600
  1.9 0.0 copy-start.1
  1.9 1.2 %copy-done.1 = f32[512,512]{1,0:T(8,128)S(1)} copy-done((f32[512,512]{1,0:T(8,128)S(1)}, f32[512,512]{1,0:T(8,128)}, u32[]{:S(2)}) %copy-start.1) | copy-done | bytes 1048600
  3.1 0.0 copy-start.2
  3.1 1.2 %copy-done.2 = f32[512,512]{1,0:T(8,128)S(1)} copy-done((f32[512,512]{1,0:T(8,128)S(1)}, f32[512,512]{1,0:T(8,128)}, u32[]{:S(2)}) %copy-start.2) | copy-done | bytes 1048600
  4.3 0.0 copy-start.3
  4.3 0.7 copy-done.3
  5.0 63.6 %perceiver.1 = (f32[512,512]{1,0:T(8,128)S(1)}, f32[512,512]{1,0:T(8,128)S(1)}) custom-call(f32[512,512]{1,0:T(8,128)S(1)} %copy-done, f32[512,512]{1,0:T(8,128)S(1)} %copy-done.1, f32[512,512]{1,0:T(8,128)S(1)} %copy-done.2, f32[1,512]{1,0:T(1,128)S(1)} %bitcast.1, f32[512,512]{1,0:T(8,128)} %wk_in.1, f32[512,512]{1,0:T(8,128)} %wv_in.1, f32[512,512]{1,0:T(8,128)} %q_in.1), custom_call_target="tpu_custom_call" | custom-call | tf_op jit(solution)/shard_map/perceiver/pallas_call | solution.py:288
  68.6 1.0 %copy.11 = f32[512,512]{1,0:T(8,128)} copy(f32[512,512]{1,0:T(8,128)S(1)} %get-tuple-element.4) | data formatting | bytes 2097152
  69.6 1.0 %copy.12 = f32[512,512]{1,0:T(8,128)} copy(f32[512,512]{1,0:T(8,128)S(1)} %get-tuple-element.5) | data formatting | bytes 2097152
Async XLA Ops:
  0.6 1.2 %copy-start = (f32[512,512]{1,0:T(8,128)S(1)}, f32[512,512]{1,0:T(8,128)}, u32[]{:S(2)}) copy-start(f32[512,512]{1,0:T(8,128)} %lat_in.1) | copy-start | bytes 3145732
  1.9 1.2 %copy-start.1 = (f32[512,512]{1,0:T(8,128)S(1)}, f32[512,512]{1,0:T(8,128)}, u32[]{:S(2)}) copy-start(f32[512,512]{1,0:T(8,128)} %keys_in.1) | copy-start | bytes 3145732
  3.1 1.2 %copy-start.2 = (f32[512,512]{1,0:T(8,128)S(1)}, f32[512,512]{1,0:T(8,128)}, u32[]{:S(2)}) copy-start(f32[512,512]{1,0:T(8,128)} %vals_in.1) | copy-start | bytes 3145732
  4.3 0.7 copy-start.3

commit v2 on v1

--- a/solution.py
+++ b/solution.py
@@ -21,6 +21,7 @@
 NN = (((1,), (0,)), ((), ()))
 NT = (((1,), (1,)), ((), ()))
 SCALE = 512.0**-0.5
+BAND = 256
 
 
 def split(value):
@@ -40,7 +41,7 @@
     lat, keys, vals, gain, wk, wv, q,
     kh, kl, vh, vl, qh, ql, wvh, wvl,
     slab_send, slab_own, slab_sib, slab_c, slab_r, piece, piece_r,
-    g, acc, mx, tot, result,
+    g, acc, mx, tot,
     in_sem, out_sem, a0s, a0r, a1s, a1r, a2s, a2r, g1s, g1r, g2s, g2r, g3s, g3r, cs, cr,
 ):
     p = lax.axis_index("pix")
@@ -212,72 +213,111 @@
         second["y", d].wait_recv()
         second["x", d].wait_recv()
 
-    def low_of(xx, cc):
-        return g.at[xx, pl.ds(pl.multiple_of(cc * HALF, HALF), 128)]
-
-    def high_of(yy, cc):
-        return g.at[:, pl.ds(pl.multiple_of(cc * HALF + 128 + yy * 32, 32), 32)]
-
+    def low_of(xx, cc, part):
+        first, count = {"all": (0, 128), "A": (0, 64), "B": (64, 64)}[part]
+        return g.at[xx, pl.ds(pl.multiple_of(cc * HALF + first, 64), count)]
+
+    def high_of(yy, cc, part):
+        blocks = {"all": pl.ds(0, 4), "A": pl.ds(0, 2), "B": pl.ds(2, 2)}[part]
+        return g.at[blocks, pl.ds(pl.multiple_of(cc * HALF + 128 + yy * 32, 32), 32)]
+
+    def source(axis, d, cc, part):
+        if axis == "x":
+            return low_of(lax.rem(x - d + NX, NX), cc, part)
+        return high_of(lax.rem(y - d + NY, NY), cc, part)
+
+    slots = {}
+    for axis in "xy":
+        for d, part in ((1, "A"), (3, "B"), (1, "B"), (3, "A"), (2, "A"), (2, "B")):
+            slots[axis, d, part] = len(slots)
     third = {}
-    for d in near:
-        third["x", d] = send(low_of(x, c), low_of(x, c), g3s.at[0, d], g3r.at[0, d], xpeer(d))
-        third["y", d] = send(high_of(y, c), high_of(y, c), g3s.at[1, d], g3r.at[1, d], ypeer(d))
-
-    acc[...] = jnp.zeros_like(acc)
-    tot[...] = jnp.zeros_like(tot)
+
+    def push(axis, back, d, part):
+        step = (d - back) % 4
+        k = slots[axis, d, part]
+        ref = source(axis, back, c, part)
+        third[axis, d, part] = send(
+            ref, ref, g3s.at[k], g3r.at[k], xpeer(step) if axis == "x" else ypeer(step)
+        )
+
+    for d, part in ((1, "A"), (3, "B"), (1, "B"), (3, "A")):
+        for axis in "xy":
+            push(axis, 0, d, part)
+
+    def wide(value, times):
+        return jnp.concatenate([value] * times, axis=1)
 
     def attend(blocks, start):
         n = jnp.concatenate([b.reshape(-1, D) for b in blocks], axis=0)
         n = n * (1.0 / jnp.sqrt(jnp.mean(n * n, axis=1, keepdims=True) + 1e-6))
         nh = split(n)
-        s = dot3((qh[...], ql[...]), nh, NT)
-        top = jnp.max(s, axis=1, keepdims=True)
-        if start:
-            m = top
-            w = jnp.exp(s - m)
-            tot[...] = jnp.broadcast_to(jnp.sum(w, axis=1, keepdims=True), tot.shape)
-            acc[...] = dot3(split(w), nh, NN)
-        else:
-            old = mx[:, 0:1]
-            m = jnp.maximum(old, top)
-            w = jnp.exp(s - m)
-            fade = jnp.exp(old - m)
-            tot[...] = tot[...] * fade + jnp.sum(w, axis=1, keepdims=True)
-            acc[...] = acc[...] * fade + dot3(split(w), nh, NN)
-        mx[...] = jnp.broadcast_to(m, mx.shape)
-
-    def source(kind, d, cc):
-        if kind == "x":
-            return low_of(lax.rem(x - d + NX, NX), cc)
-        return high_of(lax.rem(y - d + NY, NY), cc)
-
-    steps = [("x", 0), ("y", 0), ("x", 1), ("y", 1), ("x", 3), ("y", 3), ("x", 2), ("y", 2)]
-
-    def forward(k):
-        kind, d = steps[k]
-        if d:
-            third[kind, d].wait_recv()
-        ref = source(kind, d, c)
-        return send(ref, ref, cs.at[k], cr.at[k], sib)
-
-    forwards = {0: forward(0), 1: forward(1)}
-    for k, (kind, d) in enumerate(steps):
-        if k >= 1 and k + 1 < len(steps):
-            forwards[k + 1] = forward(k + 1)
-        forwards[k].wait_recv()
-        if k == len(steps) - 1:
-            save = pltpu.make_async_copy(g.at[x], state_out, out_sem.at[0])
-            save.start()
-        attend([source(kind, d, 0)[...], source(kind, d, 1)[...]], k == 0)
-
-    o = acc[...] / tot[:, 0:1] * gain[...]
-    result[...] = dot3(split(o), (wvh[...], wvl[...]), NN)
-    write = pltpu.make_async_copy(result, pix_out, out_sem.at[1])
-    write.start()
+        bands = [slice(r, r + BAND) for r in range(0, ROWS, BAND)]
+
+        def scores(band):
+            return dot3((qh[band, :], ql[band, :]), nh, NT)
+
+        ahead = scores(bands[0])
+        for k, band in enumerate(bands):
+            s = ahead
+            if k + 1 < len(bands):
+                ahead = scores(bands[k + 1])
+            columns = s.shape[1] // 128
+            top = jnp.broadcast_to(jnp.max(s, axis=1, keepdims=True), (BAND, 128))
+            m = top if start else jnp.maximum(mx[band, :], top)
+            w = jnp.exp(s - wide(m, columns))
+            total = functools.reduce(jnp.add, [w[:, t * 128 : (t + 1) * 128] for t in range(columns)])
+            read = dot3(split(w), nh, NN)
+            if not start:
+                fade = jnp.exp(mx[band, :] - m)
+                total = tot[band, :] * fade + total
+                read = acc[band, :] * wide(fade, TILES) + read
+            mx[band, :] = m
+            tot[band, :] = total
+            acc[band, :] = read
+
+    chunks = [
+        [("x", 0, "all"), ("y", 0, "all")],
+        [("x", 1, "A"), ("y", 1, "A"), ("x", 3, "B"), ("y", 3, "B")],
+        [("x", 1, "B"), ("y", 1, "B"), ("x", 3, "A"), ("y", 3, "A")],
+        [("x", 2, "A"), ("x", 2, "B"), ("y", 2, "A"), ("y", 2, "B")],
+    ]
+    passed = {}
+
+    def pass_on(chunk):
+        for axis, d, part in chunk:
+            if d:
+                third[axis, d, part].wait_recv()
+            if (d, part) == (1, "A"):
+                push(axis, 1, 2, "A")
+            if (d, part) == (3, "B"):
+                push(axis, 3, 2, "B")
+            ref = source(axis, d, c, part)
+            k = len(passed)
+            passed[axis, d, part] = send(ref, ref, cs.at[k], cr.at[k], sib)
+
+    def use(chunk, start=False):
+        for item in chunk:
+            passed[item].wait_recv()
+        attend([source(axis, d, cc, part)[...] for axis, d, part in chunk for cc in range(2)], start)
+
+    pass_on(chunks[0])
+    use(chunks[0], True)
+    pass_on(chunks[1])
+    pass_on(chunks[2])
+    use(chunks[1])
+    use(chunks[2])
+    pass_on(chunks[3])
+    for item in chunks[3]:
+        passed[item].wait_recv()
+    save = pltpu.make_async_copy(g.at[x], state_out, out_sem.at[0])
+    save.start()
+    attend([source(axis, d, cc, part)[...] for axis, d, part in chunks[3] for cc in range(2)], False)
+
+    o = acc[...] / jnp.sum(tot[...], axis=1, keepdims=True) * gain[...]
+    pix_out[...] = dot3(split(o), (wvh[...], wvl[...]), NN)
     for cp in started:
         cp.wait_send()
     save.wait()
-    write.wait()
 
 
 def shards(latents, pixel_keys, pixel_values, norm_gain, w_key, w_value, pixel_queries):
@@ -289,7 +329,7 @@
         kernel,
         out_shape=(jax.ShapeDtypeStruct((ROWS, D), F32), jax.ShapeDtypeStruct((ROWS, D), F32)),
         in_specs=[in_hbm] * 7,
-        out_specs=(in_hbm, in_hbm),
+        out_specs=(pl.BlockSpec(memory_space=pltpu.VMEM),) * 2,
         scratch_shapes=[
             big, big, big, pltpu.VMEM((1, D), F32), big, big, big,
             half, half, half, half, half, half, half, half,
@@ -304,15 +344,14 @@
             big,
             pltpu.VMEM((ROWS, 128), F32),
             pltpu.VMEM((ROWS, 128), F32),
-            big,
-            dma((7,)), dma((2,)),
+            dma((7,)), dma((1,)),
             dma((NY,)), dma((NY,)), dma((NY,)), dma((NY,)),
             dma((NZ,)), dma((NZ,)), dma((NZ,)), dma((NZ,)),
-            dma((2, NY)), dma((2, NY)), dma((2, NY)), dma((2, NY)),
-            dma((8,)), dma((8,)),
+            dma((2, NY)), dma((2, NY)), dma((12,)), dma((12,)),
+            dma((14,)), dma((14,)),
         ],
         compiler_params=pltpu.CompilerParams(
-            collective_id=0, has_side_effects=True, vmem_limit_bytes=48 << 20
+            collective_id=0, has_side_effects=True, vmem_limit_bytes=60 << 20
         ),
         name="perceiver",
     )(latents, pixel_keys, pixel_values, norm_gain.reshape(1, D), w_key, w_value, pixel_queries)

time: 70.8 us -> 59.3 us (0.84)
  Pallas kernels: 63.6 us -> 55.2 us
  local copies, waits for them, and re-layouts: 6.29 us -> 3.32 us
    pallas_call x1, Pallas kernels: 63.6 us -> 55.2 us  [shards(): pl.pallas_call(kernel, out_shape=(jax.ShapeDtypeStruct((ROWS, D), F32), j...]
    unnamed x10 -> x4, local copies, waits for them, and re-layouts: 6.29 us -> 3.32 us
where the time goes in v2:
time: 59.3 us; the launch traced here: 59.2 us
  Pallas kernels  55.2 us (93%)
  local copies, waits for them, and re-layouts  3.32 us (6%)
  between operations  0.65 us (1%)
    pallas_call x1, Pallas kernels, shards(): pl.pallas_call(kernel, out_shape=(jax.ShapeDtypeStruct((ROWS, D), F32), j...  55.2 us
    unnamed x4, local copies, waits for them, and re-layouts  3.32 us

profile of v2, /device:TPU:1, one launch (start us, length us, event | category | flops | bytes accessed | tf_op | source)
XLA Modules:
  0.0 59.2 jit_solution(12104567892317750529)
XLA Ops:
  0.6 55.2 %perceiver.1 = (f32[512,512]{1,0:T(8,128)}, f32[512,512]{1,0:T(8,128)}) custom-call(f32[512,512]{1,0:T(8,128)} %lat_in.1, f32[512,512]{1,0:T(8,128)} %keys_in.1, f32[512,512]{1,0:T(8,128)} %vals_in.1, f32[1,512]{1,0:T(1,128)} %bitcast.1, f32[512,512]{1,0:T(8,128)} %wk_in.1, f32[512,512]{1,0:T(8,128)} %wv_in.1, f32[512,512]{1,0:T(8,128)} %q_in.1), custom_call_target="tpu_custom_call" | custom-call | tf_op jit(solution)/shard_map/perceiver/pallas_call | solution.py:328
  55.8 0.0 copy-start
  55.8 2.4 %copy.11 = f32[512,512]{1,0:T(8,128)} copy(f32[512,512]{1,0:T(8,128)} %get-tuple-element.4) | data formatting | bytes 2097152
  58.2 0.0 copy-done
  58.2 1.0 %copy.12 = f32[512,512]{1,0:T(8,128)} copy(f32[512,512]{1,0:T(8,128)S(1)} %copy-done) | data formatting | bytes 2097152
Async XLA Ops:
  55.8 2.4 %copy-start = (f32[512,512]{1,0:T(8,128)S(1)}, f32[512,512]{1,0:T(8,128)}, u32[]{:S(2)}) copy-start(f32[512,512]{1,0:T(8,128)} %get-tuple-element.5) | copy-start | bytes 3145732

commit v3 on v2

--- a/solution.py
+++ b/solution.py
@@ -16,7 +16,7 @@
 GROUP = 8
 TILES = D // 128
 SLAB = TILES * NZ * GROUP + 16
-PIECE = TILES * GROUP + 16
+PIECE = TILES * GROUP + 8
 TOP = TILES * NZ * GROUP
 NN = (((1,), (0,)), ((), ()))
 NT = (((1,), (1,)), ((), ()))
@@ -101,9 +101,11 @@
     loads[1].wait()
     kh[...], kl[...] = split(keys[...])
 
-    def first(which, slab):
+    def first_scores(which):
         lh = split(lat[pl.ds(pl.multiple_of(which * HALF, HALF), HALF), :])
-        s = dot3(lh, (kh[...], kl[...]), NT) * SCALE
+        return dot3(lh, (kh[...], kl[...]), NT) * SCALE
+
+    def first_read(s, slab):
         top = jnp.max(s, axis=1, keepdims=True)
         w = jnp.exp(s - top)
         total = jnp.sum(w, axis=1, keepdims=True)
@@ -122,16 +124,18 @@
             slab[yy, TOP : TOP + 8, :] = tops
             slab[yy, TOP + 8 : TOP + 16, :] = totals
 
+    away = first_scores(1 - c)
     loads[2].wait()
     vh[...], vl[...] = split(vals[...])
-    first(1 - c, slab_send)
+    here = first_scores(c)
+    first_read(away, slab_send)
     pl.semaphore_wait(barrier, len(peers))
-    order = (1, 3, 2, 0)
+    order = (2, 1, 3, 0)
     siblings = {}
     for d in order:
         yy = lax.rem(y + d, NY)
         siblings[d] = send(slab_send.at[yy], slab_sib.at[yy], a0s.at[d], a0r.at[d], sib)
-    first(c, slab_own)
+    first_read(here, slab_own)
 
     to_y = {}
     for d in order:
@@ -173,8 +177,7 @@
             piece[zz, t * GROUP : (t + 1) * GROUP, :] = functools.reduce(
                 jnp.add, [u * v[r : r + GROUP, :] for u, v in zip(cols, parts)]
             )
-        piece[zz, TILES * GROUP : TILES * GROUP + 8, :] = jnp.broadcast_to(m[:, zz : zz + 1], (8, 128))
-        piece[zz, TILES * GROUP + 8 : PIECE, :] = jnp.broadcast_to(total[:, zz : zz + 1], (8, 128))
+        piece[zz, TILES * GROUP : PIECE, :] = jnp.where(lanes < 64, m[:, zz : zz + 1], total[:, zz : zz + 1])
 
     z_order = (4, 3, 5, 2, 6, 1, 7)
     to_z = {}
@@ -186,10 +189,11 @@
     for d in z_order:
         to_z[d].wait_recv()
     parts = [piece.at[z]] + [piece_r.at[d] for d in range(1, NZ)]
-    tops = [v[TILES * GROUP : TILES * GROUP + 8, :] for v in parts]
+    stats = [v[TILES * GROUP : PIECE, :] for v in parts]
+    tops = [v[:, 0:1] for v in stats]
     m = functools.reduce(jnp.maximum, tops)
     scales = [jnp.exp(v - m) for v in tops]
-    total = functools.reduce(jnp.add, [s * v[TILES * GROUP + 8 : PIECE, :] for s, v in zip(scales, parts)])
+    total = functools.reduce(jnp.add, [s * v[:, 64:65] for s, v in zip(scales, stats)])
     row = pl.multiple_of(c * HALF + (z // 4) * 128 + y * 32 + lax.rem(z, 4) * GROUP, GROUP)
     for t in range(TILES):
         o = functools.reduce(
@@ -209,9 +213,6 @@
     for d in near:
         second["y", d] = send(low, low, g2s.at[0, d], g2r.at[0, d], ypeer(d))
         second["x", d] = send(high, high, g2s.at[1, d], g2r.at[1, d], xpeer(d))
-    for d in near:
-        second["y", d].wait_recv()
-        second["x", d].wait_recv()
 
     def low_of(xx, cc, part):
         first, count = {"all": (0, 128), "A": (0, 64), "B": (64, 64)}[part]
@@ -240,14 +241,18 @@
             ref, ref, g3s.at[k], g3r.at[k], xpeer(step) if axis == "x" else ypeer(step)
         )
 
-    for d, part in ((1, "A"), (3, "B"), (1, "B"), (3, "A")):
-        for axis in "xy":
+    earlier = len(started)
+    for axis, before in (("x", "y"), ("y", "x")):
+        for d in near:
+            second[before, d].wait_recv()
+        for d, part in ((1, "A"), (3, "B"), (1, "B"), (3, "A")):
             push(axis, 0, d, part)
 
     def wide(value, times):
         return jnp.concatenate([value] * times, axis=1)
 
-    def attend(blocks, start):
+    def attend(chunk, start=False, last=False):
+        blocks = [source(axis, d, cc, part)[...] for axis, d, part in chunk for cc in range(2)]
         n = jnp.concatenate([b.reshape(-1, D) for b in blocks], axis=0)
         n = n * (1.0 / jnp.sqrt(jnp.mean(n * n, axis=1, keepdims=True) + 1e-6))
         nh = split(n)
@@ -271,9 +276,13 @@
                 fade = jnp.exp(mx[band, :] - m)
                 total = tot[band, :] * fade + total
                 read = acc[band, :] * wide(fade, TILES) + read
-            mx[band, :] = m
-            tot[band, :] = total
-            acc[band, :] = read
+            if last:
+                o = read / jnp.sum(total, axis=1, keepdims=True) * gain[...]
+                pix_out[band, :] = dot3(split(o), (wvh[...], wvl[...]), NN)
+            else:
+                mx[band, :] = m
+                tot[band, :] = total
+                acc[band, :] = read
 
     chunks = [
         [("x", 0, "all"), ("y", 0, "all")],
@@ -295,32 +304,36 @@
             k = len(passed)
             passed[axis, d, part] = send(ref, ref, cs.at[k], cr.at[k], sib)
 
-    def use(chunk, start=False):
+    def wait_for(chunk):
         for item in chunk:
             passed[item].wait_recv()
-        attend([source(axis, d, cc, part)[...] for axis, d, part in chunk for cc in range(2)], start)
 
     pass_on(chunks[0])
-    use(chunks[0], True)
+    wait_for(chunks[0])
+    attend(chunks[0], start=True)
+    for cp in started[:earlier]:
+        cp.wait_send()
     pass_on(chunks[1])
     pass_on(chunks[2])
-    use(chunks[1])
-    use(chunks[2])
+    sent = len(started)
+    wait_for(chunks[1])
+    attend(chunks[1])
+    wait_for(chunks[2])
+    attend(chunks[2])
+    for cp in started[earlier:sent]:
+        cp.wait_send()
     pass_on(chunks[3])
-    for item in chunks[3]:
-        passed[item].wait_recv()
+    wait_for(chunks[3])
     save = pltpu.make_async_copy(g.at[x], state_out, out_sem.at[0])
     save.start()
-    attend([source(axis, d, cc, part)[...] for axis, d, part in chunks[3] for cc in range(2)], False)
-
-    o = acc[...] / jnp.sum(tot[...], axis=1, keepdims=True) * gain[...]
-    pix_out[...] = dot3(split(o), (wvh[...], wvl[...]), NN)
-    for cp in started:
+    attend(chunks[3], last=True)
+    for cp in started[sent:]:
         cp.wait_send()
     save.wait()
 
 
 def shards(latents, pixel_keys, pixel_values, norm_gain, w_key, w_value, pixel_queries):
+    operands = (latents, pixel_keys, pixel_values, norm_gain.reshape(1, D), w_key, w_value, pixel_queries)
     in_hbm = pl.BlockSpec(memory_space=pltpu.HBM)
     big = pltpu.VMEM((ROWS, D), F32)
     half = pltpu.VMEM((ROWS, D), BF16)
@@ -351,10 +364,10 @@
             dma((14,)), dma((14,)),
         ],
         compiler_params=pltpu.CompilerParams(
-            collective_id=0, has_side_effects=True, vmem_limit_bytes=60 << 20
+            collective_id=0, has_side_effects=True, vmem_limit_bytes=50 << 20
         ),
         name="perceiver",
-    )(latents, pixel_keys, pixel_values, norm_gain.reshape(1, D), w_key, w_value, pixel_queries)
+    )(*(pltpu.with_memory_space_constraint(v, pltpu.HBM) for v in operands))
 
 
 def solution(mesh):

time: 59.3 us -> 55.7 us (0.939)
  Pallas kernels: 55.2 us -> 53 us
  local copies, waits for them, and re-layouts: 3.32 us -> 1.94 us
    pallas_call x1, Pallas kernels: 55.2 us -> 53 us  [shards(): pl.pallas_call(kernel, out_shape=(jax.ShapeDtypeStruct((ROWS, D), F32), j...]
    unnamed x4 -> x2, local copies, waits for them, and re-layouts: 3.32 us -> 1.94 us
where the time goes in v3:
time: 55.7 us; the launch traced here: 55.6 us
  Pallas kernels  53 us (95%)
  local copies, waits for them, and re-layouts  1.94 us (3%)
  between operations  0.64 us (1%)
    pallas_call x1, Pallas kernels, shards(): pl.pallas_call(kernel, out_shape=(jax.ShapeDtypeStruct((ROWS, D), F32), j...  53 us
    unnamed x2, local copies, waits for them, and re-layouts  1.94 us

profile of v3, /device:TPU:1, one launch (start us, length us, event | category | flops | bytes accessed | tf_op | source)
XLA Modules:
  0.0 55.6 jit_solution(8827212077868612621)
XLA Ops:
  0.6 53.0 %perceiver.1 = (f32[512,512]{1,0:T(8,128)S(1)}, f32[512,512]{1,0:T(8,128)S(1)}) custom-call(f32[512,512]{1,0:T(8,128)} %lat_in.1, f32[512,512]{1,0:T(8,128)} %keys_in.1, f32[512,512]{1,0:T(8,128)} %vals_in.1, f32[1,512]{1,0:T(1,128)} %bitcast.1, f32[512,512]{1,0:T(8,128)} %wk_in.1, f32[512,512]{1,0:T(8,128)} %wv_in.1, f32[512,512]{1,0:T(8,128)} %q_in.1), custom_call_target="tpu_custom_call" | custom-call | tf_op jit(solution)/shard_map/perceiver/pallas_call | solution.py:341
  53.7 1.0 %copy.11 = f32[512,512]{1,0:T(8,128)} copy(f32[512,512]{1,0:T(8,128)S(1)} %get-tuple-element.4) | data formatting | bytes 2097152
  54.6 1.0 %copy.12 = f32[512,512]{1,0:T(8,128)} copy(f32[512,512]{1,0:T(8,128)S(1)} %get-tuple-element.5) | data formatting | bytes 2097152

commit v4 on v3

--- a/solution.py
+++ b/solution.py
@@ -37,9 +37,9 @@
 
 
 def kernel(
-    lat_in, keys_in, vals_in, gain_in, wk_in, wv_in, q_in, state_out, pix_out,
+    lat_in, keys_in, vals_in, gain_in, wk_in, wv_in, q_in, state_out, read_out, wvh, wvl,
     lat, keys, vals, gain, wk, wv, q,
-    kh, kl, vh, vl, qh, ql, wvh, wvl,
+    kh, kl, vh, vl, qh, ql,
     slab_send, slab_own, slab_sib, slab_c, slab_r, piece, piece_r,
     g, acc, mx, tot,
     in_sem, out_sem, a0s, a0r, a1s, a1r, a2s, a2r, g1s, g1r, g2s, g2r, g3s, g3r, cs, cr,
@@ -68,9 +68,9 @@
     for k, (src, dst) in enumerate(
         [(lat_in, lat), (keys_in, keys), (vals_in, vals), (q_in, q), (wk_in, wk), (gain_in, gain), (wv_in, wv)]
     ):
-        cp = pltpu.make_async_copy(src, dst, in_sem.at[k])
+        loads.append(pltpu.make_async_copy(src, dst, in_sem.at[k]))
+    for cp in loads[:3]:
         cp.start()
-        loads.append(cp)
 
     barrier = pltpu.get_barrier_semaphore()
     peers = (
@@ -89,10 +89,11 @@
 
     started = []
 
-    def send(*args):
+    def send(*args, keep=True):
         cp = remote(*args)
         cp.start()
-        started.append(cp)
+        if keep:
+            started.append(cp)
         return cp
 
     lanes = lax.broadcasted_iota(jnp.int32, (GROUP, 128), 1)
@@ -126,6 +127,8 @@
 
     away = first_scores(1 - c)
     loads[2].wait()
+    for cp in loads[3:]:
+        cp.start()
     vh[...], vl[...] = split(vals[...])
     here = first_scores(c)
     first_read(away, slab_send)
@@ -238,7 +241,7 @@
         k = slots[axis, d, part]
         ref = source(axis, back, c, part)
         third[axis, d, part] = send(
-            ref, ref, g3s.at[k], g3r.at[k], xpeer(step) if axis == "x" else ypeer(step)
+            ref, ref, g3s.at[k], g3r.at[k], xpeer(step) if axis == "x" else ypeer(step),
         )
 
     earlier = len(started)
@@ -277,8 +280,7 @@
                 total = tot[band, :] * fade + total
                 read = acc[band, :] * wide(fade, TILES) + read
             if last:
-                o = read / jnp.sum(total, axis=1, keepdims=True) * gain[...]
-                pix_out[band, :] = dot3(split(o), (wvh[...], wvl[...]), NN)
+                read_out[band, :] = read / jnp.sum(total, axis=1, keepdims=True) * gain[...]
             else:
                 mx[band, :] = m
                 tot[band, :] = total
@@ -318,11 +320,11 @@
     sent = len(started)
     wait_for(chunks[1])
     attend(chunks[1])
+    pass_on(chunks[3])
     wait_for(chunks[2])
     attend(chunks[2])
     for cp in started[earlier:sent]:
         cp.wait_send()
-    pass_on(chunks[3])
     wait_for(chunks[3])
     save = pltpu.make_async_copy(g.at[x], state_out, out_sem.at[0])
     save.start()
@@ -332,20 +334,35 @@
     save.wait()
 
 
+def last(read, state, high, low, state_out, pix_out, buffer, sem):
+    copies = [pltpu.make_async_copy(state, state_out, sem.at[0])]
+    copies[0].start()
+    for k in range(2):
+        rows = pl.ds(k * HALF, HALF)
+        buffer[rows, :] = dot3(split(read[rows, :]), (high[...], low[...]), NN)
+        cp = pltpu.make_async_copy(buffer.at[rows], pix_out.at[rows], sem.at[1 + k])
+        cp.start()
+        copies.append(cp)
+    for cp in copies:
+        cp.wait()
+
+
 def shards(latents, pixel_keys, pixel_values, norm_gain, w_key, w_value, pixel_queries):
     operands = (latents, pixel_keys, pixel_values, norm_gain.reshape(1, D), w_key, w_value, pixel_queries)
     in_hbm = pl.BlockSpec(memory_space=pltpu.HBM)
     big = pltpu.VMEM((ROWS, D), F32)
     half = pltpu.VMEM((ROWS, D), BF16)
     dma = pltpu.SemaphoreType.DMA
-    return pl.pallas_call(
+    whole, rounded = jax.ShapeDtypeStruct((ROWS, D), F32), jax.ShapeDtypeStruct((D, D), BF16)
+    in_vmem = pl.BlockSpec(memory_space=pltpu.VMEM)
+    state, read, high, low = pl.pallas_call(
         kernel,
-        out_shape=(jax.ShapeDtypeStruct((ROWS, D), F32), jax.ShapeDtypeStruct((ROWS, D), F32)),
+        out_shape=(whole, whole, rounded, rounded),
         in_specs=[in_hbm] * 7,
-        out_specs=(pl.BlockSpec(memory_space=pltpu.VMEM),) * 2,
+        out_specs=(in_vmem,) * 4,
         scratch_shapes=[
             big, big, big, pltpu.VMEM((1, D), F32), big, big, big,
-            half, half, half, half, half, half, half, half,
+            half, half, half, half, half, half,
             pltpu.VMEM((NY, SLAB, 128), F32),
             pltpu.VMEM((NY, SLAB, 128), F32),
             pltpu.VMEM((NY, SLAB, 128), F32),
@@ -368,6 +385,15 @@
         ),
         name="perceiver",
     )(*(pltpu.with_memory_space_constraint(v, pltpu.HBM) for v in operands))
+    return pl.pallas_call(
+        last,
+        out_shape=(whole, whole),
+        in_specs=[in_vmem] * 4,
+        out_specs=(in_hbm, in_hbm),
+        scratch_shapes=[big, dma((3,))],
+        compiler_params=pltpu.CompilerParams(vmem_limit_bytes=16 << 20),
+        name="values",
+    )(read, state, high, low)
 
 
 def solution(mesh):

time: 55.7 us -> 54.3 us (0.975)
  local copies, waits for them, and re-layouts: 1.94 us -> 0 us
    unnamed x2 -> x0, local copies, waits for them, and re-layouts: 1.94 us -> none
    pallas_call x1 -> x2, Pallas kernels: 53 us -> 53.6 us  [the longest x1 51.7 us: shards(): pl.pallas_call(kernel, out_shape=(whole, whole, rounded, rounded), in_spe...]
where the time goes in v4:
time: 54.3 us; the launch traced here: 54.2 us
  Pallas kernels  53.5 us (99%)
  between operations  0.64 us (1%)
    pallas_call x1, Pallas kernels, shards(): pl.pallas_call(kernel, out_shape=(whole, whole, rounded, rounded), in_spe...  51.7 us
    pallas_call x1, Pallas kernels, shards(): pl.pallas_call(last, out_shape=(whole, whole), in_specs=[in_vmem] * 4, ou...  1.81 us

profile of v4, /device:TPU:1, one launch (start us, length us, event | category | flops | bytes accessed | tf_op | source)
XLA Modules:
  0.0 54.2 jit_solution(17911296720546264289)
XLA Ops:
  0.6 51.7 %perceiver.1 = (f32[512,512]{1,0:T(8,128)S(1)}, f32[512,512]{1,0:T(8,128)S(1)}, bf16[512,512]{1,0:T(8,128)(2,1)S(1)}, bf16[512,512]{1,0:T(8,128)(2,1)S(1)}) custom-call(f32[512,512]{1,0:T(8,128)} %lat_in.1, f32[512,512]{1,0:T(8,128)} %keys_in.1, f32[512,512]{1,0:T(8,128)} %vals_in.1, f32[1,512]{1,0:T(1,128)} %bitcast.1, f32[512,512]{1,0:T(8,128)} %wk_in.1, ...), custom_call_target="tpu_custom_call" | custom-call | tf_op jit(solution)/shard_map/perceiver/pallas_call | solution.py:358
  52.4 1.8 %values.1 = (f32[512,512]{1,0:T(8,128)}, f32[512,512]{1,0:T(8,128)}) custom-call(f32[512,512]{1,0:T(8,128)S(1)} %get-tuple-element.6.read, f32[512,512]{1,0:T(8,128)S(1)} %get-tuple-element.7.state, bf16[512,512]{1,0:T(8,128)(2,1)S(1)} %get-tuple-element.8.high, bf16[512,512]{1,0:T(8,128)(2,1)S(1)} %get-tuple-element.9.low), custom_call_target="tpu_custom_call" | custom-call | tf_op jit(solution)/shard_map/values/pallas_call | solution.py:388

commit v5 on v4

--- a/solution.py
+++ b/solution.py
@@ -15,15 +15,21 @@
 HALF = ROWS // 2
 GROUP = 8
 TILES = D // 128
-SLAB = TILES * NZ * GROUP + 16
-PIECE = TILES * GROUP + 8
-TOP = TILES * NZ * GROUP
+PIECE = TILES * GROUP + 1
+PART = TILES * NZ // 2 * GROUP
+TOPS, TOTALS = slice(PART, PART + 8), slice(PART + 8, PART + 16)
+SLAB = 2 * PART + 16
 NN = (((1,), (0,)), ((), ()))
 NT = (((1,), (1,)), ((), ()))
 SCALE = 512.0**-0.5
 BAND = 256
 
 
+def tile_of(t, zz):
+    r = (zz // 4) * (PART + 16) + (t * 4 + zz % 4) * GROUP
+    return slice(r, r + GROUP)
+
+
 def split(value):
     high = value.astype(BF16)
     return high, (value - high.astype(F32)).astype(BF16)
@@ -40,7 +46,7 @@
     lat_in, keys_in, vals_in, gain_in, wk_in, wv_in, q_in, state_out, read_out, wvh, wvl,
     lat, keys, vals, gain, wk, wv, q,
     kh, kl, vh, vl, qh, ql,
-    slab_send, slab_own, slab_sib, slab_c, slab_r, piece, piece_r,
+    slab_send, slab_own, slab_sib, slab_far, slab_r, piece, piece_r,
     g, acc, mx, tot,
     in_sem, out_sem, a0s, a0r, a1s, a1r, a2s, a2r, g1s, g1r, g2s, g2r, g3s, g3r, cs, cr,
 ):
@@ -97,6 +103,7 @@
         return cp
 
     lanes = lax.broadcasted_iota(jnp.int32, (GROUP, 128), 1)
+    sublanes = lax.broadcasted_iota(jnp.int32, (GROUP, 128), 0)
 
     loads[0].wait()
     loads[1].wait()
@@ -119,11 +126,9 @@
                 tops = jnp.where(lanes == zz, top[r : r + GROUP], tops)
                 totals = jnp.where(lanes == zz, total[r : r + GROUP], totals)
                 for t in range(TILES):
-                    slab[yy, (t * NZ + zz) * GROUP : (t * NZ + zz + 1) * GROUP, :] = o[
-                        r : r + GROUP, t * 128 : (t + 1) * 128
-                    ]
-            slab[yy, TOP : TOP + 8, :] = tops
-            slab[yy, TOP + 8 : TOP + 16, :] = totals
+                    slab[yy, tile_of(t, zz), :] = o[r : r + GROUP, t * 128 : (t + 1) * 128]
+            slab[yy, TOPS, :] = tops
+            slab[yy, TOTALS, :] = totals
 
     away = first_scores(1 - c)
     loads[2].wait()
@@ -140,47 +145,76 @@
         siblings[d] = send(slab_send.at[yy], slab_sib.at[yy], a0s.at[d], a0r.at[d], sib)
     first_read(here, slab_own)
 
-    to_y = {}
-    for d in order:
+    def merge(into, d, tops, totals, others, zs, mask=None):
+        old, new = into[d, TOPS, :], tops
+        if mask is not None:
+            new = jnp.where(mask, new, old)
+        m = jnp.maximum(old, new)
+        a, b = jnp.exp(old - m), jnp.exp(new - m)
+        added = b * totals
+        if mask is not None:
+            added = jnp.where(mask, added, 0.0)
+        into[d, TOPS, :] = m
+        into[d, TOTALS, :] = a * into[d, TOTALS, :] + added
+        for zz in zs:
+            az, bz = a[:, zz : zz + 1], b[:, zz : zz + 1]
+            for t in range(TILES):
+                r = tile_of(t, zz)
+                into[d, r, :] = az * into[d, r, :] + bz * others(r)
+
+    def own_slab(d):
         yy = lax.rem(y + d, NY)
         siblings[d].wait_recv()
-        mo, ms = slab_own[yy, TOP : TOP + 8, :], slab_sib[yy, TOP : TOP + 8, :]
-        m = jnp.maximum(mo, ms)
-        a, b = jnp.exp(mo - m), jnp.exp(ms - m)
-        slab_c[d, TOP : TOP + 8, :] = m
-        slab_c[d, TOP + 8 : TOP + 16, :] = (
-            a * slab_own[yy, TOP + 8 : TOP + 16, :] + b * slab_sib[yy, TOP + 8 : TOP + 16, :]
-        )
-        for zz in range(NZ):
-            az, bz = a[:, zz : zz + 1], b[:, zz : zz + 1]
-            for t in range(TILES):
-                r = (t * NZ + zz) * GROUP
-                slab_c[d, r : r + GROUP, :] = (
-                    az * slab_own[yy, r : r + GROUP, :] + bz * slab_sib[yy, r : r + GROUP, :]
-                )
-        if d:
-            to_y[d] = send(slab_c.at[d], slab_r.at[d], a1s.at[d], a1r.at[d], ypeer(d))
+        merge(
+            slab_own, yy, slab_sib[yy, TOPS, :], slab_sib[yy, TOTALS, :], lambda r: slab_sib[yy, r, :], range(NZ)
+        )
+        return yy
+
+    front, back = pl.ds(0, PART + 16), pl.ds(PART, PART + 16)
+    front_only, back_only = pl.ds(0, PART), pl.ds(PART + 16, PART)
+    two_on = own_slab(2)
+    through = (
+        send(slab_own.at[two_on, front], slab_far.at[0, front], a1s.at[0], a1r.at[0], ypeer(1)),
+        send(slab_own.at[two_on, back], slab_far.at[1, back], a1s.at[1], a1r.at[1], ypeer(3)),
+    )
+    to_y = []
+    after = own_slab(1)
+    to_y.append(send(slab_own.at[after, back_only], slab_r.at[1, back_only], a1s.at[2], a1r.at[2], ypeer(1)))
+    before = own_slab(3)
+    to_y.append(send(slab_own.at[before, front_only], slab_r.at[3, front_only], a1s.at[3], a1r.at[3], ypeer(3)))
+    for k, (yy, zs, mask, rows, slot, d) in enumerate(
+        ((after, range(4), lanes < 4, front, 1, 1), (before, range(4, NZ), lanes >= 4, back, 3, 3))
+    ):
+        through[k].wait_recv()
+        merge(
+            slab_own, yy, slab_far[k, TOPS, :], slab_far[k, TOTALS, :], lambda r, k=k: slab_far[k, r, :], zs, mask
+        )
+        to_y.append(send(slab_own.at[yy, rows], slab_r.at[slot, rows], a1s.at[4 + k], a1r.at[4 + k], ypeer(d)))
+    own_slab(0)
 
     for k in (3, 4, 5):
         loads[k].wait()
     scaled = dot3(split(q[...]), split(wk[...]), NT) * (gain[...] * SCALE)
     qh[...], ql[...] = split(scaled)
 
-    for d in (1, 3, 2):
-        to_y[d].wait_recv()
-    parts = [slab_c.at[0]] + [slab_r.at[d] for d in range(1, NY)]
-    tops = [s[TOP : TOP + 8, :] for s in parts]
+    for cp in to_y:
+        cp.wait_recv()
+    parts = [slab_own.at[y], slab_r.at[1], slab_r.at[3]]
+    tops = [s[TOPS, :] for s in parts]
     m = functools.reduce(jnp.maximum, tops)
     scales = [jnp.exp(v - m) for v in tops]
-    total = functools.reduce(jnp.add, [s * v[TOP + 8 : TOP + 16, :] for s, v in zip(scales, parts)])
+    total = functools.reduce(jnp.add, [s * v[TOTALS, :] for s, v in zip(scales, parts)])
     for zz in range(NZ):
         cols = [s[:, zz : zz + 1] for s in scales]
         for t in range(TILES):
-            r = (t * NZ + zz) * GROUP
+            r = tile_of(t, zz)
             piece[zz, t * GROUP : (t + 1) * GROUP, :] = functools.reduce(
-                jnp.add, [u * v[r : r + GROUP, :] for u, v in zip(cols, parts)]
+                jnp.add, [u * v[r, :] for u, v in zip(cols, parts)]
             )
-        piece[zz, TILES * GROUP : PIECE, :] = jnp.where(lanes < 64, m[:, zz : zz + 1], total[:, zz : zz + 1])
+        both = jnp.where(lanes < GROUP, m[:, zz : zz + 1], total[:, zz : zz + 1])
+        piece[zz, TILES * GROUP : PIECE, :] = jnp.sum(
+            jnp.where(lax.rem(lanes, GROUP) == sublanes, both, 0.0), axis=0, keepdims=True
+        )
 
     z_order = (4, 3, 5, 2, 6, 1, 7)
     to_z = {}
@@ -192,11 +226,12 @@
     for d in z_order:
         to_z[d].wait_recv()
     parts = [piece.at[z]] + [piece_r.at[d] for d in range(1, NZ)]
-    stats = [v[TILES * GROUP : PIECE, :] for v in parts]
-    tops = [v[:, 0:1] for v in stats]
+    stats = [jnp.broadcast_to(v[TILES * GROUP : PIECE, :], (GROUP, 128)) for v in parts]
+    tops = [jnp.sum(jnp.where(lanes == sublanes, v, 0.0), axis=1, keepdims=True) for v in stats]
+    totals = [jnp.sum(jnp.where(lanes == sublanes + GROUP, v, 0.0), axis=1, keepdims=True) for v in stats]
     m = functools.reduce(jnp.maximum, tops)
     scales = [jnp.exp(v - m) for v in tops]
-    total = functools.reduce(jnp.add, [s * v[:, 64:65] for s, v in zip(scales, stats)])
+    total = functools.reduce(jnp.add, [s * v for s, v in zip(scales, totals)])
     row = pl.multiple_of(c * HALF + (z // 4) * 128 + y * 32 + lax.rem(z, 4) * GROUP, GROUP)
     for t in range(TILES):
         o = functools.reduce(
@@ -254,8 +289,8 @@
     def wide(value, times):
         return jnp.concatenate([value] * times, axis=1)
 
-    def attend(chunk, start=False, last=False):
-        blocks = [source(axis, d, cc, part)[...] for axis, d, part in chunk for cc in range(2)]
+    def attend(chunk, cores, start=False, last=False):
+        blocks = [source(axis, d, cc, part)[...] for axis, d, part in chunk for cc in cores]
         n = jnp.concatenate([b.reshape(-1, D) for b in blocks], axis=0)
         n = n * (1.0 / jnp.sqrt(jnp.mean(n * n, axis=1, keepdims=True) + 1e-6))
         nh = split(n)
@@ -310,25 +345,26 @@
         for item in chunk:
             passed[item].wait_recv()
 
+    near = chunks[1] + chunks[2]
+    far = chunks[3]
     pass_on(chunks[0])
     wait_for(chunks[0])
-    attend(chunks[0], start=True)
+    attend(chunks[0], (0, 1), start=True)
     for cp in started[:earlier]:
         cp.wait_send()
-    pass_on(chunks[1])
-    pass_on(chunks[2])
+    pass_on(near)
     sent = len(started)
-    wait_for(chunks[1])
-    attend(chunks[1])
-    pass_on(chunks[3])
-    wait_for(chunks[2])
-    attend(chunks[2])
+    attend(near, (c,))
+    wait_for(near)
+    attend(near, (1 - c,))
+    pass_on(far)
+    attend(far, (c,))
     for cp in started[earlier:sent]:
         cp.wait_send()
-    wait_for(chunks[3])
+    wait_for(far)
     save = pltpu.make_async_copy(g.at[x], state_out, out_sem.at[0])
     save.start()
-    attend(chunks[3], last=True)
+    attend(far, (1 - c,), last=True)
     for cp in started[sent:]:
         cp.wait_send()
     save.wait()
@@ -366,7 +402,7 @@
             pltpu.VMEM((NY, SLAB, 128), F32),
             pltpu.VMEM((NY, SLAB, 128), F32),
             pltpu.VMEM((NY, SLAB, 128), F32),
-            pltpu.VMEM((NY, SLAB, 128), F32),
+            pltpu.VMEM((2, SLAB, 128), F32),
             pltpu.VMEM((NY, SLAB, 128), F32),
             pltpu.VMEM((NZ, PIECE, 128), F32),
             pltpu.VMEM((NZ, PIECE, 128), F32),
@@ -375,7 +411,7 @@
             pltpu.VMEM((ROWS, 128), F32),
             pltpu.VMEM((ROWS, 128), F32),
             dma((7,)), dma((1,)),
-            dma((NY,)), dma((NY,)), dma((NY,)), dma((NY,)),
+            dma((NY,)), dma((NY,)), dma((6,)), dma((6,)),
             dma((NZ,)), dma((NZ,)), dma((NZ,)), dma((NZ,)),
             dma((2, NY)), dma((2, NY)), dma((12,)), dma((12,)),
             dma((14,)), dma((14,)),

time: 54.3 us -> 54 us (level)
  no operation moved by 1% of the time
where the time goes in v5:
time: 54 us; the launch traced here: 53.9 us
  Pallas kernels  53.2 us (99%)
  between operations  0.64 us (1%)
    pallas_call x1, Pallas kernels, shards(): pl.pallas_call(kernel, out_shape=(whole, whole, rounded, rounded), in_spe...  51.4 us
    pallas_call x1, Pallas kernels, shards(): pl.pallas_call(last, out_shape=(whole, whole), in_specs=[in_vmem] * 4, ou...  1.81 us

profile of v5, /device:TPU:1, one launch (start us, length us, event | category | flops | bytes accessed | tf_op | source)
XLA Modules:
  0.0 53.9 jit_solution(7655309602405404500)
XLA Ops:
  0.6 51.4 %perceiver.1 = (f32[512,512]{1,0:T(8,128)S(1)}, f32[512,512]{1,0:T(8,128)S(1)}, bf16[512,512]{1,0:T(8,128)(2,1)S(1)}, bf16[512,512]{1,0:T(8,128)(2,1)S(1)}) custom-call(f32[512,512]{1,0:T(8,128)} %lat_in.1, f32[512,512]{1,0:T(8,128)} %keys_in.1, f32[512,512]{1,0:T(8,128)} %vals_in.1, f32[1,512]{1,0:T(1,128)} %bitcast.1, f32[512,512]{1,0:T(8,128)} %wk_in.1, ...), custom_call_target="tpu_custom_call" | custom-call | tf_op jit(solution)/shard_map/perceiver/pallas_call | solution.py:394
  52.1 1.8 %values.1 = (f32[512,512]{1,0:T(8,128)}, f32[512,512]{1,0:T(8,128)}) custom-call(f32[512,512]{1,0:T(8,128)S(1)} %get-tuple-element.6.read, f32[512,512]{1,0:T(8,128)S(1)} %get-tuple-element.7.state, bf16[512,512]{1,0:T(8,128)(2,1)S(1)} %get-tuple-element.8.high, bf16[512,512]{1,0:T(8,128)(2,1)S(1)} %get-tuple-element.9.low), custom_call_target="tpu_custom_call" | custom-call | tf_op jit(solution)/shard_map/values/pallas_call | solution.py:424

commit v6 on v5

--- a/solution.py
+++ b/solution.py
@@ -246,7 +246,7 @@
         gather_z[d].wait_recv()
     low = g.at[x, pl.ds(pl.multiple_of(c * HALF + y * 32, 32), 32)]
     high = g.at[x, pl.ds(pl.multiple_of(c * HALF + 128 + y * 32, 32), 32)]
-    near = (1, 3, 2)
+    near = (2, 1, 3)
     second = {}
     for d in near:
         second["y", d] = send(low, low, g2s.at[0, d], g2r.at[0, d], ypeer(d))
@@ -348,10 +348,10 @@
     near = chunks[1] + chunks[2]
     far = chunks[3]
     pass_on(chunks[0])
+    for cp in started[:earlier]:
+        cp.wait_send()
     wait_for(chunks[0])
     attend(chunks[0], (0, 1), start=True)
-    for cp in started[:earlier]:
-        cp.wait_send()
     pass_on(near)
     sent = len(started)
     attend(near, (c,))

time: 54 us -> 53.2 us (0.985)
  Pallas kernels: 53.2 us -> 52.4 us
    pallas_call x1, Pallas kernels: 51.4 us -> 50.6 us  [shards(): pl.pallas_call(kernel, out_shape=(whole, whole, rounded, rounded), in_spe...]
where the time goes in v6:
time: 53.2 us; the launch traced here: 53.1 us
  Pallas kernels  52.4 us (98%)
  between operations  0.64 us (1%)
    pallas_call x1, Pallas kernels, shards(): pl.pallas_call(kernel, out_shape=(whole, whole, rounded, rounded), in_spe...  50.6 us
    pallas_call x1, Pallas kernels, shards(): pl.pallas_call(last, out_shape=(whole, whole), in_specs=[in_vmem] * 4, ou...  1.81 us

profile of v6, /device:TPU:1, one launch (start us, length us, event | category | flops | bytes accessed | tf_op | source)
XLA Modules:
  0.0 53.1 jit_solution(4419652422416121778)
XLA Ops:
  0.6 50.6 %perceiver.1 = (f32[512,512]{1,0:T(8,128)S(1)}, f32[512,512]{1,0:T(8,128)S(1)}, bf16[512,512]{1,0:T(8,128)(2,1)S(1)}, bf16[512,512]{1,0:T(8,128)(2,1)S(1)}) custom-call(f32[512,512]{1,0:T(8,128)} %lat_in.1, f32[512,512]{1,0:T(8,128)} %keys_in.1, f32[512,512]{1,0:T(8,128)} %vals_in.1, f32[1,512]{1,0:T(1,128)} %bitcast.1, f32[512,512]{1,0:T(8,128)} %wk_in.1, ...), custom_call_target="tpu_custom_call" | custom-call | tf_op jit(solution)/shard_map/perceiver/pallas_call | solution.py:394
  51.3 1.8 %values.1 = (f32[512,512]{1,0:T(8,128)}, f32[512,512]{1,0:T(8,128)}) custom-call(f32[512,512]{1,0:T(8,128)S(1)} %get-tuple-element.6.read, f32[512,512]{1,0:T(8,128)S(1)} %get-tuple-element.7.state, bf16[512,512]{1,0:T(8,128)(2,1)S(1)} %get-tuple-element.8.high, bf16[512,512]{1,0:T(8,128)(2,1)S(1)} %get-tuple-element.9.low), custom_call_target="tpu_custom_call" | custom-call | tf_op jit(solution)/shard_map/values/pallas_call | solution.py:424

commit v7 on v6

--- a/solution.py
+++ b/solution.py
@@ -352,15 +352,17 @@
         cp.wait_send()
     wait_for(chunks[0])
     attend(chunks[0], (0, 1), start=True)
-    pass_on(near)
+    pass_on(chunks[1])
+    attend(chunks[1], (c,))
+    pass_on(chunks[2])
     sent = len(started)
-    attend(near, (c,))
+    attend(chunks[2], (c,))
     wait_for(near)
     attend(near, (1 - c,))
+    for cp in started[earlier:sent]:
+        cp.wait_send()
     pass_on(far)
     attend(far, (c,))
-    for cp in started[earlier:sent]:
-        cp.wait_send()
     wait_for(far)
     save = pltpu.make_async_copy(g.at[x], state_out, out_sem.at[0])
     save.start()

time: 53.2 us -> 52.5 us (0.987)
  Pallas kernels: 52.4 us -> 51.8 us
    pallas_call x1, Pallas kernels: 50.6 us -> 50 us  [shards(): pl.pallas_call(kernel, out_shape=(whole, whole, rounded, rounded), in_spe...]
where the time goes in v7:
time: 52.5 us
  Pallas kernels  51.8 us (99%)
  between operations  0.64 us (1%)
    pallas_call x1, Pallas kernels, shards(): pl.pallas_call(kernel, out_shape=(whole, whole, rounded, rounded), in_spe...  50 us
    pallas_call x1, Pallas kernels, shards(): pl.pallas_call(last, out_shape=(whole, whole), in_specs=[in_vmem] * 4, ou...  1.81 us

profile of v7, /device:TPU:1, one launch (start us, length us, event | category | flops | bytes accessed | tf_op | source)
XLA Modules:
  0.0 52.5 jit_solution(15921764396531896102)
XLA Ops:
  0.6 50.0 %perceiver.1 = (f32[512,512]{1,0:T(8,128)S(1)}, f32[512,512]{1,0:T(8,128)S(1)}, bf16[512,512]{1,0:T(8,128)(2,1)S(1)}, bf16[512,512]{1,0:T(8,128)(2,1)S(1)}) custom-call(f32[512,512]{1,0:T(8,128)} %lat_in.1, f32[512,512]{1,0:T(8,128)} %keys_in.1, f32[512,512]{1,0:T(8,128)} %vals_in.1, f32[1,512]{1,0:T(1,128)} %bitcast.1, f32[512,512]{1,0:T(8,128)} %wk_in.1, ...), custom_call_target="tpu_custom_call" | custom-call | tf_op jit(solution)/shard_map/perceiver/pallas_call | solution.py:396
  50.6 1.8 %values.1 = (f32[512,512]{1,0:T(8,128)}, f32[512,512]{1,0:T(8,128)}) custom-call(f32[512,512]{1,0:T(8,128)S(1)} %get-tuple-element.6.read, f32[512,512]{1,0:T(8,128)S(1)} %get-tuple-element.7.state, bf16[512,512]{1,0:T(8,128)(2,1)S(1)} %get-tuple-element.8.high, bf16[512,512]{1,0:T(8,128)(2,1)S(1)} %get-tuple-element.9.low), custom_call_target="tpu_custom_call" | custom-call | tf_op jit(solution)/shard_map/values/pallas_call | solution.py:426
